TPU v7x, 32 devices: a whole 2x2x4 slice. The times are simulated.
32 devices in a mesh: pole: 4 (over y, x), row: 2 (over core), col: 4 (over z).
Axes of the slice: x: 2, y: 2, z: 4, core: 2. Of those that a mesh axis runs over, the one named last changes fastest.
Arguments:
- hamiltonian_panel: bfloat16 [6144, 512], P(('row', 'col'), 'pole'), may hold values from -0.005859375 to 0.005859375
- margin_panel: bfloat16 [6144, 512], P(('row', 'col'), 'pole'), may hold values from -0.0029296875 to 0.0029296875
- shifts: float32 [4, 2], P('pole'), may hold values from -2 to 2
- weights: float32 [4, 2], P('pole'), may hold values from 0.5 to 2
- pivot_inverse: float32 [4, 2, 512, 512], P('pole'), may hold values from -6 to 6
- selected_inverse: bfloat16 [4, 2, 6144, 6144], P('pole', None, 'row', 'col'), may hold values from -6 to 6
Outputs:
- inverse_column: float32 [4, 6144, 2, 512], P('pole', ('row', 'col'))
- inverse_pivot: float32 [4, 2, 512, 512], P('pole')
- density_column: float32 [6144, 512], P(('row', 'col'), 'pole')
- density_pivot: float32 [512, 512], P('pole')
All inputs are finite; a program needn't handle non-finite values.
Results may differ from a plain program's by a relative error of at most 0.0037.
Values may be sent and summed in bfloat16 or wider, within the bound.
A program may use at most 128 MiB of HBM per device.

v0:
```python
import jax
import jax.numpy as jnp
from jax import lax
from jax.sharding import PartitionSpec as P

HALVES = 2


def precise(left, right):
    return jnp.dot(left, right, precision=lax.Precision.HIGH, preferred_element_type=jnp.float32)


def gather_panel(pair):
    return lax.all_gather(pair, "pole", axis=2, tiled=True)


def factor_panel(pair, shift, inverse):
    hamiltonian_f = pair[0].astype(jnp.float32)
    margin_f = pair[1].astype(jnp.float32)
    real_part = hamiltonian_f - shift[0] * margin_f
    imag_part = -shift[1] * margin_f
    lower_real = precise(real_part, inverse[0]) - precise(imag_part, inverse[1])
    lower_imag = precise(real_part, inverse[1]) + precise(imag_part, inverse[0])
    return (lower_real.astype(jnp.bfloat16), lower_imag.astype(jnp.bfloat16))


def half_dot(left, right):
    return lax.dot_general(
        left, right, (((0,), (0,)), ((), ())), preferred_element_type=jnp.float32
    )


def body(hamiltonian_panel, margin_panel, shifts, weights, pivot_inverse, selected_inverse):
    shift = shifts[0]
    weight = weights[0]
    inverse = pivot_inverse[0]
    block_real = selected_inverse[0, 0]
    block_imag = selected_inverse[0, 1]
    n_row = lax.axis_size("row")
    n_col = lax.axis_size("col")
    n_pole = lax.axis_size("pole")
    width = inverse.shape[-1]
    part = width // HALVES
    own_pair = jnp.stack([hamiltonian_panel, margin_panel])
    order = [(n_row * c + r, r * n_col + c) for r in range(n_row) for c in range(n_col)]
    met_pair = gather_panel(lax.ppermute(own_pair, ("row", "col"), order))
    met_real, met_imag = factor_panel(met_pair, shift, inverse)
    partials = []
    for h in range(HALVES):
        cut = slice(h * part, (h + 1) * part)
        mine = jnp.concatenate([met_real[:, cut], met_imag[:, cut]], axis=1)
        rows = lax.all_gather(mine, "row", axis=0, tiled=True)
        turned = jnp.concatenate([rows[:, part:], -rows[:, :part]], axis=1)
        total = jnp.dot(block_imag, turned, preferred_element_type=jnp.float32) - jnp.dot(
            block_real, rows, preferred_element_type=jnp.float32
        )
        partials.append(total.astype(jnp.bfloat16))
    own_pair, partials[-1] = lax.optimization_barrier((own_pair, partials[-1]))
    own_real, own_imag = factor_panel(gather_panel(own_pair), shift, inverse)
    lower = jnp.concatenate([own_real, own_imag], axis=1)
    columns = []
    updates = []
    for h in range(HALVES):
        column = lax.psum_scatter(partials[h], "col", scatter_dimension=0, tiled=True).astype(
            jnp.float32
        )
        high = column.astype(jnp.bfloat16)
        low = (column - high.astype(jnp.float32)).astype(jnp.bfloat16)
        square = half_dot(lower, high) + half_dot(lower, low)
        update = jnp.stack(
            [
                square[:width, :part] - square[width:, part:],
                square[:width, part:] + square[width:, :part],
            ]
        )
        updates.append(lax.psum(update, ("row", "col")))
        columns.append(column.reshape(column.shape[0], 2, part))
    column = jnp.concatenate(columns, axis=2)
    pivot = inverse - jnp.concatenate(updates, axis=2)
    column_density = weight[0] * column[:, 0] - weight[1] * column[:, 1]
    share = width // n_pole
    pieces = column_density.reshape(-1, n_pole, share).swapaxes(0, 1).astype(jnp.bfloat16)
    column_share = jnp.sum(
        lax.all_to_all(pieces, "pole", 0, 0, tiled=True).astype(jnp.float32), axis=0
    )
    pivot_density = weight[0] * pivot[0] - weight[1] * pivot[1]
    pieces = pivot_density.reshape(n_pole, share, width).astype(jnp.bfloat16)
    pivot_share = jnp.sum(
        lax.all_to_all(pieces, "pole", 0, 0, tiled=True).astype(jnp.float32), axis=0
    )
    return (column[None], pivot[None], column_share, pivot_share)


def solution(mesh):
    return jax.shard_map(
        body,
        mesh=mesh,
        in_specs=(
            P(("row", "col"), "pole"),
            P(("row", "col"), "pole"),
            P("pole", None),
            P("pole", None),
            P("pole", None, None, None),
            P("pole", None, "row", "col"),
        ),
        out_specs=(
            P("pole", ("row", "col"), None, None),
            P("pole", None, None, None),
            P(("row", "col"), "pole"),
            P("pole", None),
        ),
        check_vma=False,
    )
```

profile of v0, /device:TPU:0, one launch (start us, length us, event | category | flops | bytes accessed | tf_op | source)
XLA Modules:
  0.0 350.2 jit_solution(6100513097827890616)
XLA Ops:
  7.2 0.0 all-gather.5.cloned.1.call-start
  7.2 1.1 pad_maximum_fusion.6
  8.3 0.7 collective-permute-start
  9.0 0.7 copy-done.17
  9.8 0.0 all-gather.9.cloned.1.call-start
  9.8 1.3 fusion.112
  11.8 42.8 %all-gather.5.cloned.1.call-done = bf16[2,768,512]{2,1,0:T(8,128)(2,1)} async-done(((bf16[2,768,128]{2,1,0:T(8,128)(2,1)}), bf16[2,768,512]{2,1,0:T(8,128)(2,1)}) %all-gather.5.cloned.1.call-update) | async-done | bytes 1572880 | tf_op jit(solution)/shard_map/all_gather | solution.py:14
  54.6 3.2 fusion.28
  57.9 2.9 fusion.26
  60.7 2.3 subtract_convert_fusion.5
  63.0 2.3 add_convert_fusion.1
  65.3 0.1 fusion.109
  65.4 0.9 pad_maximum_fusion.5
  66.4 0.0 all-gather.7.cloned.1.call-start
  66.4 1.0 pad_maximum_fusion.4
  67.4 0.0 all-gather.11.cloned.1.call-start
  67.5 8.9 %all-gather.9.cloned.1.call-done = bf16[1536,512]{0,1:T(8,128)(2,1)} async-done(((bf16[768,512]{0,1:T(8,128)(2,1)}), bf16[1536,512]{0,1:T(8,128)(2,1)}) %all-gather.9.cloned.1.call-update) | async-done | bytes 1572880 | tf_op jit(solution)/shard_map/all_gather | solution.py:52
  76.3 9.2 %fusion = f32[512,3072]{1,0:T(8,128)S(1)} fusion(bf16[1536,512]{0,1:T(8,128)(2,1)} %all-gather.9.cloned.1.call-done, bf16[1,2,3072,1536]{3,2,1,0:T(8,128)(2,1)} %param.11), kind=kOutput, calls=%fused_computation | convolution fusion | flops 4831838208 | bytes 17301504 | tf_op jit(solution)/shard_map/dot_general | solution.py:54
  85.6 0.1 fusion.108
  85.7 11.0 %fusion.19 = bf16[3072,512]{0,1:T(8,128)(2,1)} fusion(f32[512,3072]{1,0:T(8,128)S(1)} %fusion, bf16[1,2,3072,1536]{3,2,1,0:T(8,128)(2,1)} %param.11, bf16[1536,256]{0,1:T(8,128)(2,1)S(1)} %get-tuple-element.25, bf16[1536,256]{0,1:T(8,128)(2,1)S(1)} %get-tuple-element.24), kind=kOutput, calls=%fused_computation.20 | convolution fusion | flops 4838129664 | bytes 20447232 | tf_op jit(solution)/shard_map/dot_general | solution.py:54
  96.7 0.0 reduce-scatter.5.cloned.1.call-start
  96.7 0.5 reduce-scatter.5.cloned.1.call-update
  97.3 0.2 reduce-scatter.3.cloned.1.call-start
  97.5 0.0 all-gather.7.cloned.1.call-done
  97.5 1.6 fusion.107
  99.1 0.3 copy-done.6
  99.4 7.7 %fusion.2 = f32[512,3072]{1,0:T(8,128)S(1)} fusion(bf16[1536,512]{0,1:T(8,128)(2,1)S(1)} %copy-done.6, bf16[1,2,3072,1536]{3,2,1,0:T(8,128)(2,1)} %param.11), kind=kOutput, calls=%fused_computation.2 | convolution fusion | flops 4831838208 | bytes 17301504 | tf_op jit(solution)/shard_map/dot_general | solution.py:54
  107.1 10.6 %fusion.16 = bf16[3072,512]{0,1:T(8,128)(2,1)} fusion(f32[512,3072]{1,0:T(8,128)S(1)} %fusion.2, bf16[1,2,3072,1536]{3,2,1,0:T(8,128)(2,1)} %param.11, bf16[1536,256]{0,1:T(8,128)(2,1)S(1)} %get-tuple-element.23, bf16[1536,256]{0,1:T(8,128)(2,1)S(1)} %get-tuple-element.22), kind=kOutput, calls=%fused_computation.19 | convolution fusion | flops 4838129664 | bytes 20447232 | tf_op jit(solution)/shard_map/dot_general | solution.py:54
  117.7 0.0 all-reduce.3.cloned.1.call-start
  117.7 11.2 %all-gather.11.cloned.1.call-done = bf16[2,768,512]{2,1,0:T(8,128)(2,1)} async-done(((bf16[2,768,128]{2,1,0:T(8,128)(2,1)}), bf16[2,768,512]{2,1,0:T(8,128)(2,1)}) %all-gather.11.cloned.1.call-update) | async-done | bytes 1572880 | tf_op jit(solution)/shard_map/all_gather | solution.py:14
  128.9 3.7 %fusion.53 = f32[768,512]{0,1:T(8,128)S(1)} fusion(f32[1,2,512,512]{3,2,1,0:T(8,128)S(1)} %copy-done, f32[]{:T(128)} %bitcast.2, bf16[2,768,512]{2,1,0:T(8,128)(2,1)} %all-gather.11.cloned.1.call-done), kind=kOutput, calls=%fused_computation.60 | convolution fusion | flops 1209532416 | bytes 4194308 | tf_op jit(solution)/shard_map/dot_general | solution.py:10
  132.6 2.3 fusion.55
  134.9 1.6 add_convert_fusion
  136.6 2.5 subtract_convert_fusion.4
  139.1 52.8 %reduce-scatter.5.cloned.1.call-done = bf16[768,512]{0,1:T(8,128)(2,1)} async-done(((bf16[3072,512]{0,1:T(8,128)(2,1)}), bf16[768,512]{0,1:T(8,128)(2,1)}) %reduce-scatter.5.cloned.1.call-update) | async-done | bytes 786448 | tf_op jit(solution)/shard_map/reduce_scatter | solution.py:64
  191.9 2.5 fusion.105
  194.4 1.0 convolution_add_fusion
  195.5 0.1 fusion.90
  195.6 58.8 %reduce-scatter.3.cloned.1.call-done = bf16[768,512]{0,1:T(8,128)(2,1)} async-done(((bf16[3072,512]{0,1:T(8,128)(2,1)}), bf16[768,512]{0,1:T(8,128)(2,1)}) %reduce-scatter.3.cloned.1.call-update) | async-done | bytes 786448 | tf_op jit(solution)/shard_map/reduce_scatter | solution.py:64
  254.4 2.8 fusion.106
  257.2 1.0 convolution_add_fusion.1
  258.2 0.1 fusion.92
  258.3 1.1 pad_maximum_fusion.3
  259.4 1.1 pad_maximum_fusion.2
  260.5 0.6 copy-done.18
  261.2 0.6 fusion.111
  261.8 0.1 convert
  261.9 0.5 copy-done.16
  262.4 0.1 convert.1
  262.5 0.5 copy-done.1
  263.0 1.1 copy-done.2
  264.2 1.8 fusion.22
  266.0 5.7 %copy.13 = f32[1,768,2,512]{3,2,1,0:T(2,128)} copy(f32[1,768,2,512]{1,3,2,0:T(8,128)} %fusion.22) | data formatting | bytes 6291456
  271.7 4.3 %fusion.40 = bf16[768,1,512]{0,2,1:T(8,128)(2,1)} fusion(f32[768,2,256]{0,2,1:T(8,128)} %copy-done.2, f32[768,2,256]{0,2,1:T(8,128)} %copy-done.1, f32[]{:T(128)} %bitcast.24, f32[]{:T(128)} %bitcast.23), kind=kLoop, calls=%fused_computation.43 | loop fusion | flops 2359296 | bytes 3932168 | tf_op jit(solution)/shard_map/convert_element_type | solution.py:82
  276.0 4.2 %all-to-all-start = ((bf16[4,768,128]{1,2,0:T(8,128)(2,1)}), bf16[4,768,128]{1,2,0:T(8,128)(2,1)}, u32[]{:S(2)}, u32[]{:S(2)}) async-start(bf16[4,768,128]{1,2,0:T(8,128)(2,1)} %bitcast.26), calls=%async_computation.2 | async-start | bytes 1572864 | tf_op jit(solution)/shard_map/all_to_all | solution.py:84
  280.2 45.3 %all-reduce.3.cloned.1.call-done = (f32[2,512,256]{2,1,0:T(8,128)}, f32[2,512,256]{2,1,0:T(8,128)}) async-done(((f32[2,512,256]{2,1,0:T(8,128)}, f32[2,512,256]{2,1,0:T(8,128)}), (f32[2,512,256]{2,1,0:T(8,128)}, f32[2,512,256]{2,1,0:T(8,128)})) %all-reduce.3.cloned.1.call-update) | async-done | bytes 2097168 | tf_op jit(solution)/shard_map/psum | solution.py:76
  325.5 2.0 maximum_subtract_fusion.1
  327.5 2.4 fusion.60
  329.9 4.3 %all-to-all-start.1 = ((bf16[4,128,512]{2,1,0:T(8,128)(2,1)}), bf16[4,128,512]{2,1,0:T(8,128)(2,1)}, u32[]{:S(2)}, u32[]{:S(2)}) async-start(bf16[4,128,512]{2,1,0:T(8,128)(2,1)} %bitcast.94), calls=%async_computation.3 | async-start | bytes 1048576 | tf_op jit(solution)/shard_map/all_to_all | solution.py:89
  334.2 1.3 convert_reduce_fusion
  335.5 0.9 copy.14
  336.4 2.9 maximum_subtract_fusion
  339.3 2.2 all-to-all-done.1
  341.5 1.8 convert_reduce_fusion.1
  (40 shorter events, 0.2 us)
Async XLA Ops:
  7.2 47.4 %all-gather.5.cloned.1.call-start = ((), (), s32[]{:S(2)}) async-start(), calls=%async_computation.4 | async-start | bytes 1966080 | tf_op jit(solution)/shard_map/all_gather | solution.py:14
  8.3 49.6 %copy-start.8 = (bf16[2,768,128]{2,1,0:T(8,128)(2,1)}, bf16[2,768,128]{2,1,0:T(8,128)(2,1)S(1)}, u32[]{:S(2)}) copy-start(bf16[2,768,128]{2,1,0:T(8,128)(2,1)S(1)} %pad_maximum_fusion.6) | copy-start | bytes 1179652
  8.3 0.7 collective-permute-start
  9.0 0.7 copy-start.17
  9.8 66.6 %all-gather.9.cloned.1.call-start = ((), (), s32[]{:S(2)}) async-start(), calls=%async_computation.7 | async-start | bytes 2359296 | tf_op jit(solution)/shard_map/all_gather | solution.py:52
  54.6 3.2 copy-start
  57.9 2.9 copy-start.4
  66.4 31.1 %all-gather.7.cloned.1.call-start = ((), (), s32[]{:S(2)}) async-start(), calls=%async_computation.5 | async-start | bytes 2359296 | tf_op jit(solution)/shard_map/all_gather | solution.py:52
  67.4 61.5 %all-gather.11.cloned.1.call-start = ((), (), s32[]{:S(2)}) async-start(), calls=%async_computation.9 | async-start | bytes 1966080 | tf_op jit(solution)/shard_map/all_gather | solution.py:14
  76.3 9.2 %copy-start.7 = (bf16[1536,512]{0,1:T(8,128)(2,1)S(1)}, bf16[1536,512]{0,1:T(8,128)(2,1)}, u32[]{:S(2)}) copy-start(bf16[1536,512]{0,1:T(8,128)(2,1)} %all-gather.9.cloned.1.call-done) | copy-start | bytes 4718596
  96.7 95.2 %reduce-scatter.5.cloned.1.call-start = ((), (), s32[]{:S(2)}) async-start(), calls=%async_computation.8 | async-start | bytes 3932160 | tf_op jit(solution)/shard_map/reduce_scatter | solution.py:64
  97.3 157.1 %reduce-scatter.3.cloned.1.call-start = ((), (), s32[]{:S(2)}) async-start(), calls=%async_computation.6 | async-start | bytes 3932160 | tf_op jit(solution)/shard_map/reduce_scatter | solution.py:64
  97.5 1.9 copy-start.6
  117.7 207.9 %all-reduce.3.cloned.1.call-start = ((), (), s32[]{:S(2)}) async-start(), calls=%async_computation.10 | async-start | bytes 4194304 | tf_op jit(solution)/shard_map/psum | solution.py:76
  128.9 3.8 %copy-start.3 = (bf16[2,768,512]{2,1,0:T(8,128)(2,1)S(1)}, bf16[2,768,512]{2,1,0:T(8,128)(2,1)}, u32[]{:S(2)}) copy-start(bf16[2,768,512]{2,1,0:T(8,128)(2,1)} %all-gather.11.cloned.1.call-done) | copy-start | bytes 4718596
  136.6 57.8 %copy-start.9 = (bf16[768,512]{0,1:T(8,128)(2,1)}, bf16[768,512]{0,1:T(8,128)(2,1)S(1)}, u32[]{:S(2)}) copy-start(bf16[768,512]{0,1:T(8,128)(2,1)S(1)} %add_convert_fusion) | copy-start | bytes 2359300
  191.9 2.5 copy-start.11
  191.9 2.5 copy-start.13
  254.4 2.8 copy-start.10
  254.4 2.8 copy-start.12
  254.4 2.8 copy-start.15
  260.5 0.7 copy-start.18
  260.5 1.2 copy-start.14
  261.2 1.2 copy-start.16
  261.9 1.1 copy-start.1
  263.0 1.1 copy-start.2
  276.0 53.9 %all-to-all-start = ((bf16[4,768,128]{1,2,0:T(8,128)(2,1)}), bf16[4,768,128]{1,2,0:T(8,128)(2,1)}, u32[]{:S(2)}, u32[]{:S(2)}) async-start(bf16[4,768,128]{1,2,0:T(8,128)(2,1)} %bitcast.26), calls=%async_computation.2 | async-start | bytes 1572864 | tf_op jit(solution)/shard_map/all_to_all | solution.py:84
  329.9 6.5 %copy-start.5 = (f32[2,512,256]{2,1,0:T(8,128)S(1)}, f32[2,512,256]{2,1,0:T(8,128)}, u32[]{:S(2)}) copy-start(f32[2,512,256]{2,1,0:T(8,128)} %get-tuple-element.16) | copy-start | bytes 3145732
  329.9 11.6 %all-to-all-start.1 = ((bf16[4,128,512]{2,1,0:T(8,128)(2,1)}), bf16[4,128,512]{2,1,0:T(8,128)(2,1)}, u32[]{:S(2)}, u32[]{:S(2)}) async-start(bf16[4,128,512]{2,1,0:T(8,128)(2,1)} %bitcast.94), calls=%async_computation.3 | async-start | bytes 1048576 | tf_op jit(solution)/shard_map/all_to_all | solution.py:89
Sparse Core Ops, SparseCore 0:
  10.4 44.1 all-gather.4
  66.5 9.7 all-gather.8
  77.9 10.9 all-gather.6
  96.8 32.0 all-gather.10
  131.6 60.2 reduce-scatter.4
  194.0 60.2 reduce-scatter.2
  260.7 64.8 all-reduce.2
where the time goes:
time: 351 us; the launch traced here: 350 us
  waiting for transfers between devices  223 us (64%)
  matrix products  66.5 us (19%)
  other arithmetic  23.8 us (7%)
  between operations  15.1 us (4%)
  local copies, waits for them, and re-layouts  12.5 us (4%)
  starting transfers between devices  9.61 us (3%)
    reduce_scatter x2, waiting for transfers between devices, body(): lax.psum_scatter(partials[h], 'col', scatter_dimension=0, tiled=True)  112 us
    all_gather x2, waiting for transfers between devices, gather_panel(): return lax.all_gather(pair, 'pole', axis=2, tiled=True)  54 us
    psum x1, waiting for transfers between devices, body(): updates.append(lax.psum(update, ('row', 'col')))  45.3 us
    dot_general x2, matrix products, body(): jnp.dot(block_imag, turned, preferred_element_type=jnp.float32)  21.5 us
    dot_general x8, matrix products, precise(): jnp.dot(left, right, precision=lax.Precision.HIGH, preferred_element_type...  20.8 us
    dot_general x2, matrix products, body(): jnp.dot(block_real, rows, preferred_element_type=jnp.float32)  16.9 us
    unnamed x40, local copies, waits for them, and re-layouts  10.5 us
    all_gather x2, waiting for transfers between devices, body(): rows = lax.all_gather(mine, 'row', axis=0, tiled=True)  8.9 us
  transfers between devices with their start and end apart: 10, of which 7 were waited for; matrix products, arithmetic and copies ran while one was open for 22% of the time, Pallas kernels for 0%

commit v1 on v0

--- a/solution.py
+++ b/solution.py
@@ -6,12 +6,28 @@
 HALVES = 2
 
 
+def collect(x, axis, dim):
+    ways, here, lap = (lax.axis_size(axis), lax.axis_index(axis), x.shape[dim])
+    shape = [n * ways if d == dim else n for d, n in enumerate(x.shape)]
+    full = lax.dynamic_update_slice_in_dim(jnp.zeros(shape, x.dtype), x, here * lap, axis=dim)
+    going_up = going_down = x
+    for far in range(1, ways // 2 + 1):
+        going_up = lax.ppermute(going_up, axis, [(d, (d + 1) % ways) for d in range(ways)])
+        full = lax.dynamic_update_slice_in_dim(full, going_up, (here - far) % ways * lap, axis=dim)
+        if 2 * far < ways:
+            going_down = lax.ppermute(going_down, axis, [(d, (d - 1) % ways) for d in range(ways)])
+            full = lax.dynamic_update_slice_in_dim(
+                full, going_down, (here + far) % ways * lap, axis=dim
+            )
+    return full
+
+
 def precise(left, right):
     return jnp.dot(left, right, precision=lax.Precision.HIGH, preferred_element_type=jnp.float32)
 
 
 def gather_panel(pair):
-    return lax.all_gather(pair, "pole", axis=2, tiled=True)
+    return collect(pair, "pole", 2)
 
 
 def factor_panel(pair, shift, inverse):

time: 351 us -> 311 us (0.89)
  waiting for transfers between devices: 223 us -> 176 us
  starting transfers between devices: 9.61 us -> 18.5 us
  matrix products: 66.5 us -> 62.2 us
    all_gather x2 -> x0, waiting for transfers between devices: 54 us -> none  [gather_panel(): return lax.all_gather(pair, 'pole', axis=2, tiled=True)]
    reduce_scatter x2, waiting for transfers between devices: 112 us -> 62.1 us  [body(): lax.psum_scatter(partials[h], 'col', scatter_dimension=0, tiled=True)]
    ppermute x0 -> x6, waiting for transfers between devices: none -> 39.1 us  [the longest x4 29.4 us: collect(): lax.ppermute(going_up, axis, [(d, (d + 1) % ways) for d in range(ways)])]
    all_gather x2, waiting for transfers between devices: 8.9 us -> 27.6 us  [body(): rows = lax.all_gather(mine, 'row', axis=0, tiled=True)]
    ppermute x0 -> x6, starting transfers between devices: none -> 8.92 us  [the longest x4 6.73 us: collect(): lax.ppermute(going_up, axis, [(d, (d + 1) % ways) for d in range(ways)])]
    dot_general x8, matrix products: 20.8 us -> 16.5 us  [precise(): jnp.dot(left, right, precision=lax.Precision.HIGH, preferred_element_type...]
    unnamed x40 -> x32, local copies, waits for them, and re-layouts: 10.5 us -> 9.78 us
  transfers between devices with their start and end apart: 10 -> 14, of which waited for: 7 -> 11; matrix products, arithmetic and copies ran while one was open for 22% -> 25% of each run, Pallas kernels for 0% -> 0%
where the time goes in v1:
time: 311 us; the launch traced here: 310 us
  waiting for transfers between devices  176 us (57%)
  matrix products  62.2 us (20%)
  other arithmetic  23.8 us (8%)
  starting transfers between devices  18.5 us (6%)
  local copies, waits for them, and re-layouts  14.8 us (5%)
  between operations  14.8 us (5%)
    reduce_scatter x2, waiting for transfers between devices, body(): lax.psum_scatter(partials[h], 'col', scatter_dimension=0, tiled=True)  62.1 us
    psum x1, waiting for transfers between devices, body(): updates.append(lax.psum(update, ('row', 'col')))  45.2 us
    ppermute x4, waiting for transfers between devices, collect(): lax.ppermute(going_up, axis, [(d, (d + 1) % ways) for d in range(ways)])  29.4 us
    all_gather x2, waiting for transfers between devices, body(): rows = lax.all_gather(mine, 'row', axis=0, tiled=True)  27.6 us
    dot_general x2, matrix products, body(): jnp.dot(block_imag, turned, preferred_element_type=jnp.float32)  21.5 us
    dot_general x2, matrix products, body(): jnp.dot(block_real, rows, preferred_element_type=jnp.float32)  16.9 us
    dot_general x8, matrix products, precise(): jnp.dot(left, right, precision=lax.Precision.HIGH, preferred_element_type...  16.5 us
    unnamed x32, local copies, waits for them, and re-layouts  9.78 us
  transfers between devices with their start and end apart: 14, of which 11 were waited for; matrix products, arithmetic and copies ran while one was open for 25% of the time, Pallas kernels for 0%

profile of v1, /device:TPU:0, one launch (start us, length us, event | category | flops | bytes accessed | tf_op | source)
XLA Modules:
  0.0 310.4 jit_solution(1861943087635687899)
XLA Ops:
  7.2 1.1 pad_maximum_fusion.6
  8.3 0.7 collective-permute-start
  9.0 3.0 collective-permute-start.1
  12.0 1.0 collective-permute-start.2
  13.0 5.7 %collective-permute-done.1 = bf16[2,768,128]{2,1,0:T(8,128)(2,1)S(1)} collective-permute-done((bf16[2,768,128]{2,1,0:T(8,128)(2,1)S(1)}, bf16[2,768,128]{2,1,0:T(8,128)(2,1)S(1)}, u32[]{:S(2)}, u32[]{:S(2)}) %collective-permute-start.1) | collective-permute-done | bytes 393248 | tf_op jit(solution)/shard_map/ppermute | solution.py:15
  18.7 1.1 collective-permute-start.3
  19.7 1.3 fusion.106
  22.1 2.1 collective-permute-done.2
  24.2 1.1 constant_dynamic-update-slice_fusion.5
  25.3 6.4 %collective-permute-done.3 = bf16[2,768,128]{2,1,0:T(8,128)(2,1)} collective-permute-done((bf16[2,768,128]{2,1,0:T(8,128)(2,1)S(1)}, bf16[2,768,128]{2,1,0:T(8,128)(2,1)}, u32[]{:S(2)}, u32[]{:S(2)}) %collective-permute-start.3) | collective-permute-done | bytes 393248 | tf_op jit(solution)/shard_map/ppermute | solution.py:15
  31.7 1.1 constant_dynamic-update-slice_fusion.4
  32.8 1.6 fusion.28
  34.4 1.6 fusion.26
  36.0 2.3 subtract_convert_fusion.5
  38.3 2.3 add_convert_fusion.1
  40.7 0.9 pad_maximum_fusion.5
  41.7 0.9 pad_maximum_fusion.4
  42.7 0.2 reduce-scatter.5.cloned.1.call-start
  42.9 27.5 %all-gather.5.cloned.1.call-done = bf16[1536,512]{0,1:T(8,128)(2,1)} async-done(((bf16[768,512]{0,1:T(8,128)(2,1)}), bf16[1536,512]{0,1:T(8,128)(2,1)}) %all-gather.5.cloned.1.call-update) | async-done | bytes 1572880 | tf_op jit(solution)/shard_map/all_gather | solution.py:68
  70.5 9.2 %fusion = f32[512,3072]{1,0:T(8,128)S(1)} fusion(bf16[1536,512]{0,1:T(8,128)(2,1)} %all-gather.5.cloned.1.call-done, bf16[1,2,3072,1536]{3,2,1,0:T(8,128)(2,1)} %param.11), kind=kOutput, calls=%fused_computation | convolution fusion | flops 4831838208 | bytes 17301504 | tf_op jit(solution)/shard_map/dot_general | solution.py:70
  79.8 11.0 %fusion.19 = bf16[3072,512]{0,1:T(8,128)(2,1)} fusion(f32[512,3072]{1,0:T(8,128)S(1)} %fusion, bf16[1,2,3072,1536]{3,2,1,0:T(8,128)(2,1)} %param.11, bf16[1536,256]{0,1:T(8,128)(2,1)S(1)} %get-tuple-element.25, bf16[1536,256]{0,1:T(8,128)(2,1)S(1)} %get-tuple-element.24), kind=kOutput, calls=%fused_computation.20 | convolution fusion | flops 4838129664 | bytes 20447232 | tf_op jit(solution)/shard_map/dot_general | solution.py:70
  90.9 1.6 fusion.101
  92.5 0.3 copy-done.4
  92.8 7.7 %fusion.2 = f32[512,3072]{1,0:T(8,128)S(1)} fusion(bf16[1536,512]{0,1:T(8,128)(2,1)S(1)} %copy-done.4, bf16[1,2,3072,1536]{3,2,1,0:T(8,128)(2,1)} %param.11), kind=kOutput, calls=%fused_computation.2 | convolution fusion | flops 4831838208 | bytes 17301504 | tf_op jit(solution)/shard_map/dot_general | solution.py:70
  100.4 10.6 %fusion.16 = bf16[3072,512]{0,1:T(8,128)(2,1)} fusion(f32[512,3072]{1,0:T(8,128)S(1)} %fusion.2, bf16[1,2,3072,1536]{3,2,1,0:T(8,128)(2,1)} %param.11, bf16[1536,256]{0,1:T(8,128)(2,1)S(1)} %get-tuple-element.23, bf16[1536,256]{0,1:T(8,128)(2,1)S(1)} %get-tuple-element.22), kind=kOutput, calls=%fused_computation.19 | convolution fusion | flops 4838129664 | bytes 20447232 | tf_op jit(solution)/shard_map/dot_general | solution.py:70
  111.1 1.8 collective-permute-start.4
  112.9 1.2 collective-permute-start.5
  114.0 9.9 %collective-permute-done.4 = bf16[2,768,128]{2,1,0:T(8,128)(2,1)S(1)} collective-permute-done((bf16[2,768,128]{2,1,0:T(8,128)(2,1)S(1)}, bf16[2,768,128]{2,1,0:T(8,128)(2,1)S(1)}, u32[]{:S(2)}, u32[]{:S(2)}) %collective-permute-start.4) | collective-permute-done | bytes 393248 | tf_op jit(solution)/shard_map/ppermute | solution.py:15
  124.0 0.9 collective-permute-start.6
  125.1 7.6 %collective-permute-done.5 = bf16[2,768,128]{2,1,0:T(8,128)(2,1)S(1)} collective-permute-done((bf16[2,768,128]{2,1,0:T(8,128)(2,1)S(1)}, bf16[2,768,128]{2,1,0:T(8,128)(2,1)S(1)}, u32[]{:S(2)}, u32[]{:S(2)}) %collective-permute-start.5) | collective-permute-done | bytes 393248 | tf_op jit(solution)/shard_map/ppermute | solution.py:18
  132.8 7.4 %collective-permute-done.6 = bf16[2,768,128]{2,1,0:T(8,128)(2,1)S(1)} collective-permute-done((bf16[2,768,128]{2,1,0:T(8,128)(2,1)S(1)}, bf16[2,768,128]{2,1,0:T(8,128)(2,1)S(1)}, u32[]{:S(2)}, u32[]{:S(2)}) %collective-permute-start.6) | collective-permute-done | bytes 393248 | tf_op jit(solution)/shard_map/ppermute | solution.py:15
  140.3 1.6 fusion.33
  141.9 1.6 fusion.35
  143.5 2.3 add_convert_fusion
  145.8 3.2 %subtract_convert_fusion.4 = bf16[768,512]{0,1:T(8,128)(2,1)} fusion(f32[768,512]{0,1:T(8,128)S(1)} %fusion.35, f32[1,2,512,512]{3,2,1,0:T(8,128)S(1)} %copy-done, f32[]{:T(128)} %bitcast.2, bf16[2,768,512]{2,1,0:T(8,128)(2,1)S(1)} %constant_dynamic-update-slice_fusion), kind=kOutput, calls=%fused_computation.57 | convolution fusion | flops 1210318848 | bytes 4980740 | tf_op jit(solution)/shard_map/dot_general | solution.py:26
  149.0 3.4 %reduce-scatter.5.cloned.1.call-done = bf16[768,512]{0,1:T(8,128)(2,1)} async-done(((bf16[3072,512]{0,1:T(8,128)(2,1)}), bf16[768,512]{0,1:T(8,128)(2,1)}) %reduce-scatter.5.cloned.1.call-update) | async-done | bytes 786448 | tf_op jit(solution)/shard_map/reduce_scatter | solution.py:80
  152.4 2.5 fusion.99
  154.9 1.0 convolution_add_fusion
  156.0 0.1 fusion.84
  156.1 58.8 %reduce-scatter.3.cloned.1.call-done = bf16[768,512]{0,1:T(8,128)(2,1)} async-done(((bf16[3072,512]{0,1:T(8,128)(2,1)}), bf16[768,512]{0,1:T(8,128)(2,1)}) %reduce-scatter.3.cloned.1.call-update) | async-done | bytes 786448 | tf_op jit(solution)/shard_map/reduce_scatter | solution.py:80
  214.9 2.8 fusion.100
  217.7 1.0 convolution_add_fusion.1
  218.7 0.1 fusion.86
  218.8 1.1 pad_maximum_fusion.3
  219.9 1.1 pad_maximum_fusion.2
  221.1 0.6 copy-done.14
  221.7 0.6 fusion.105
  222.4 0.5 copy-done.13
  222.9 0.1 convert.1
  223.0 0.5 copy-done.1
  223.5 1.1 copy-done.2
  224.7 1.8 fusion.22
  226.5 5.7 %copy.13 = f32[1,768,2,512]{3,2,1,0:T(2,128)} copy(f32[1,768,2,512]{1,3,2,0:T(8,128)} %fusion.22) | data formatting | bytes 6291456
  232.3 4.3 %fusion.40 = bf16[768,1,512]{0,2,1:T(8,128)(2,1)} fusion(f32[768,2,256]{0,2,1:T(8,128)} %copy-done.2, f32[768,2,256]{0,2,1:T(8,128)} %copy-done.1, f32[]{:T(128)} %bitcast.24, f32[]{:T(128)} %bitcast.23), kind=kLoop, calls=%fused_computation.43 | loop fusion | flops 2359296 | bytes 3932168 | tf_op jit(solution)/shard_map/convert_element_type | solution.py:98
  236.6 4.2 %all-to-all-start = ((bf16[4,768,128]{1,2,0:T(8,128)(2,1)}), bf16[4,768,128]{1,2,0:T(8,128)(2,1)}, u32[]{:S(2)}, u32[]{:S(2)}) async-start(bf16[4,768,128]{1,2,0:T(8,128)(2,1)} %bitcast.26), calls=%async_computation.2 | async-start | bytes 1572864 | tf_op jit(solution)/shard_map/all_to_all | solution.py:100
  240.8 45.2 %all-reduce.3.cloned.1.call-done = (f32[2,512,256]{2,1,0:T(8,128)}, f32[2,512,256]{2,1,0:T(8,128)}) async-done(((f32[2,512,256]{2,1,0:T(8,128)}, f32[2,512,256]{2,1,0:T(8,128)}), (f32[2,512,256]{2,1,0:T(8,128)}, f32[2,512,256]{2,1,0:T(8,128)})) %all-reduce.3.cloned.1.call-update) | async-done | bytes 2097168 | tf_op jit(solution)/shard_map/psum | solution.py:92
  286.0 2.0 maximum_subtract_fusion.1
  288.0 2.4 fusion.54
  290.4 4.3 %all-to-all-start.1 = ((bf16[4,128,512]{2,1,0:T(8,128)(2,1)}), bf16[4,128,512]{2,1,0:T(8,128)(2,1)}, u32[]{:S(2)}, u32[]{:S(2)}) async-start(bf16[4,128,512]{2,1,0:T(8,128)(2,1)} %bitcast.90), calls=%async_computation.3 | async-start | bytes 1048576 | tf_op jit(solution)/shard_map/all_to_all | solution.py:105
  294.6 1.3 convert_reduce_fusion
  295.9 0.9 copy.14
  296.8 2.9 maximum_subtract_fusion
  299.7 2.2 all-to-all-done.1
  302.0 1.8 convert_reduce_fusion.1
  (48 shorter events, 1.4 us)
Async XLA Ops:
  7.2 63.3 %all-gather.5.cloned.1.call-start = ((), (), s32[]{:S(2)}) async-start(), calls=%async_computation.6 | async-start | bytes 2359296 | tf_op jit(solution)/shard_map/all_gather | solution.py:68
  8.3 0.7 collective-permute-start
  9.0 9.7 %collective-permute-start.1 = (bf16[2,768,128]{2,1,0:T(8,128)(2,1)S(1)}, bf16[2,768,128]{2,1,0:T(8,128)(2,1)S(1)}, u32[]{:S(2)}, u32[]{:S(2)}) collective-permute-start(bf16[2,768,128]{2,1,0:T(8,128)(2,1)S(1)} %collective-permute-done), channel_id=1, source_target_pairs={{0,8},{8,16},{16,24},{24,0},{1,9},{9,17},{17,25},{25,1},{2,10},{10... | collective-permute-start | bytes 1179656 | tf_op jit(solution)/shard_map/ppermute | solution.py:15
  12.0 12.2 %collective-permute-start.2 = (bf16[2,768,128]{2,1,0:T(8,128)(2,1)S(1)}, bf16[2,768,128]{2,1,0:T(8,128)(2,1)}, u32[]{:S(2)}, u32[]{:S(2)}) collective-permute-start(bf16[2,768,128]{2,1,0:T(8,128)(2,1)S(1)} %collective-permute-done), channel_id=1, source_target_pairs={{0,24},{8,0},{16,8},{24,16},{1,25},{9,1},{17,9},{25,17},{2,26},{10... | collective-permute-start | bytes 1179656 | tf_op jit(solution)/shard_map/ppermute | solution.py:18
  18.7 13.0 %collective-permute-start.3 = (bf16[2,768,128]{2,1,0:T(8,128)(2,1)S(1)}, bf16[2,768,128]{2,1,0:T(8,128)(2,1)}, u32[]{:S(2)}, u32[]{:S(2)}) collective-permute-start(bf16[2,768,128]{2,1,0:T(8,128)(2,1)S(1)} %collective-permute-done.1), channel_id=1, source_target_pairs={{0,8},{8,16},{16,24},{24,0},{1,9},{9,17},{17,25},{25,1},{2,10},{10... | collective-permute-start | bytes 1179656 | tf_op jit(solution)/shard_map/ppermute | solution.py:15
  21.8 10.9 %copy-start = (f32[1,2,512,512]{3,2,1,0:T(8,128)S(1)}, f32[1,2,512,512]{3,2,1,0:T(8,128)}, u32[]{:S(2)}) copy-start(f32[1,2,512,512]{3,2,1,0:T(8,128)} %param.10) | copy-start | bytes 6291460
  41.7 49.2 %all-gather.3.cloned.1.call-start = ((), (), s32[]{:S(2)}) async-start(), calls=%async_computation.4 | async-start | bytes 2359296 | tf_op jit(solution)/shard_map/all_gather | solution.py:68
  42.7 109.7 %reduce-scatter.5.cloned.1.call-start = ((), (), s32[]{:S(2)}) async-start(), calls=%async_computation.7 | async-start | bytes 3932160 | tf_op jit(solution)/shard_map/reduce_scatter | solution.py:80
  70.5 9.2 %copy-start.5 = (bf16[1536,512]{0,1:T(8,128)(2,1)S(1)}, bf16[1536,512]{0,1:T(8,128)(2,1)}, u32[]{:S(2)}) copy-start(bf16[1536,512]{0,1:T(8,128)(2,1)} %all-gather.5.cloned.1.call-done) | copy-start | bytes 4718596
  90.8 124.1 %reduce-scatter.3.cloned.1.call-start = ((), (), s32[]{:S(2)}) async-start(), calls=%async_computation.5 | async-start | bytes 3932160 | tf_op jit(solution)/shard_map/reduce_scatter | solution.py:80
  90.9 1.9 copy-start.4
  111.0 175.0 %all-reduce.3.cloned.1.call-start = ((), (), s32[]{:S(2)}) async-start(), calls=%async_computation.8 | async-start | bytes 4194304 | tf_op jit(solution)/shard_map/psum | solution.py:92
  111.1 12.9 %collective-permute-start.4 = (bf16[2,768,128]{2,1,0:T(8,128)(2,1)S(1)}, bf16[2,768,128]{2,1,0:T(8,128)(2,1)S(1)}, u32[]{:S(2)}, u32[]{:S(2)}) collective-permute-start(bf16[2,768,128]{2,1,0:T(8,128)(2,1)S(1)} %pad_maximum_fusion.6), channel_id=1, source_target_pairs={{0,8},{8,16},{16,24},{24,0},{1,9},{9,17},{17,25},{25,1},{2,10},{10... | collective-permute-start | bytes 1179656 | tf_op jit(solution)/shard_map/ppermute | solution.py:15
  112.9 19.8 %collective-permute-start.5 = (bf16[2,768,128]{2,1,0:T(8,128)(2,1)S(1)}, bf16[2,768,128]{2,1,0:T(8,128)(2,1)S(1)}, u32[]{:S(2)}, u32[]{:S(2)}) collective-permute-start(bf16[2,768,128]{2,1,0:T(8,128)(2,1)S(1)} %pad_maximum_fusion.6), channel_id=1, source_target_pairs={{0,24},{8,0},{16,8},{24,16},{1,25},{9,1},{17,9},{25,17},{2,26},{10... | collective-permute-start | bytes 1179656 | tf_op jit(solution)/shard_map/ppermute | solution.py:18
  124.0 16.2 %collective-permute-start.6 = (bf16[2,768,128]{2,1,0:T(8,128)(2,1)S(1)}, bf16[2,768,128]{2,1,0:T(8,128)(2,1)S(1)}, u32[]{:S(2)}, u32[]{:S(2)}) collective-permute-start(bf16[2,768,128]{2,1,0:T(8,128)(2,1)S(1)} %collective-permute-done.4), channel_id=1, source_target_pairs={{0,8},{8,16},{16,24},{24,0},{1,9},{9,17},{17,25},{25,1},{2,10},{10... | collective-permute-start | bytes 1179656 | tf_op jit(solution)/shard_map/ppermute | solution.py:15
  145.8 9.1 %copy-start.6 = (bf16[768,512]{0,1:T(8,128)(2,1)}, bf16[768,512]{0,1:T(8,128)(2,1)S(1)}, u32[]{:S(2)}) copy-start(bf16[768,512]{0,1:T(8,128)(2,1)S(1)} %add_convert_fusion) | copy-start | bytes 2359300
  152.4 2.5 copy-start.8
  152.4 2.5 copy-start.10
  214.9 2.8 copy-start.7
  214.9 2.8 copy-start.9
  214.9 2.8 copy-start.12
  221.0 0.7 copy-start.14
  221.0 1.2 copy-start.11
  221.7 1.2 copy-start.13
  222.4 1.2 copy-start.1
  223.5 1.1 copy-start.2
  236.6 53.8 %all-to-all-start = ((bf16[4,768,128]{1,2,0:T(8,128)(2,1)}), bf16[4,768,128]{1,2,0:T(8,128)(2,1)}, u32[]{:S(2)}, u32[]{:S(2)}) async-start(bf16[4,768,128]{1,2,0:T(8,128)(2,1)} %bitcast.26), calls=%async_computation.2 | async-start | bytes 1572864 | tf_op jit(solution)/shard_map/all_to_all | solution.py:100
  290.4 6.5 %copy-start.3 = (f32[2,512,256]{2,1,0:T(8,128)S(1)}, f32[2,512,256]{2,1,0:T(8,128)}, u32[]{:S(2)}) copy-start(f32[2,512,256]{2,1,0:T(8,128)} %get-tuple-element.16) | copy-start | bytes 3145732
  290.4 11.6 %all-to-all-start.1 = ((bf16[4,128,512]{2,1,0:T(8,128)(2,1)}), bf16[4,128,512]{2,1,0:T(8,128)(2,1)}, u32[]{:S(2)}, u32[]{:S(2)}) async-start(bf16[4,128,512]{2,1,0:T(8,128)(2,1)} %bitcast.90), calls=%async_computation.3 | async-start | bytes 1048576 | tf_op jit(solution)/shard_map/all_to_all | solution.py:105
Sparse Core Ops, SparseCore 0:
  41.8 28.6 all-gather.4
  72.0 10.9 all-gather.2
  90.9 61.4 reduce-scatter.4
  154.6 60.2 reduce-scatter.2
  221.2 64.7 all-reduce.2
